TPU v7x, 512 devices: a whole 4x8x8 slice. The times are simulated.
512 devices in a mesh: replica: 32 (over y, z_hi, core), tensor: 16 (over z_lo, x).
Axes of the slice: x: 4, y: 8, z: 8 (z_hi: 2, z_lo: 4; z = z_hi * 4 + z_lo), core: 2. Of those that a mesh axis runs over, the one named last changes fastest.
Arguments:
- trainer_weight: bfloat16 [5120, 2048], P(('replica', 'tensor')), may hold values from -0.25 to 0.25
- hidden_new: bfloat16 [512, 5120], P('replica'), may hold values from -6 to 6
- queries: bfloat16 [512, 8192], P('replica', 'tensor'), may hold values from -130 to 130
- key_cache: int32 [512, 16, 128, 128], P('replica', 'tensor'), may hold values from -128 to 127
- key_scales: float32 [512, 16, 128], P('replica', 'tensor'), may hold values from 0.005 to 0.02
- value_cache: int32 [512, 16, 128, 128], P('replica', 'tensor'), may hold values from -128 to 127
- value_scales: float32 [512, 16, 128], P('replica', 'tensor'), may hold values from 0.005 to 0.05
- lengths: int32 [512], P('replica'), may hold values from 1 to 256
Outputs:
- synced: bfloat16 [5120, 2048], P(None, 'tensor')
- block_scales: float32 [40, 16], P(None, 'tensor')
- attended: bfloat16 [512, 8192], P('replica', 'tensor')
All inputs are finite; a program needn't handle non-finite values.
Results may differ from a plain program's by a relative error of at most 0.0021.
Values may be sent and summed in bfloat16 or wider, within the bound.
A program may use at most 64 MiB of HBM per device.

v0:
```python
import math

import jax
import jax.numpy as jnp
from jax import lax
from jax.sharding import PartitionSpec as P

GROUP = 8
QB = 128


EPSILON = 1e-06
ROPE_BASE = 1000000.0
MASKED = -1e30


def swapped(array, axis, apart):
    return lax.ppermute(array, axis, [(i, i ^ 1 << apart) for i in range(lax.axis_size(axis))])


def frequencies(head_dim):
    return ROPE_BASE ** (-(jnp.arange(head_dim // 2, dtype=jnp.float32) * 2.0 / head_dim))


def rotate(vectors, angles):
    half_width = vectors.shape[-1] // 2
    cosine = jnp.cos(angles)
    sine = jnp.sin(angles)
    first = vectors[..., :half_width]
    second = vectors[..., half_width:]
    return jnp.concatenate(
        [first * cosine - second * sine, second * cosine + first * sine], axis=-1
    )


def quantize(columns):
    row_count = columns.shape[0]
    head_dim = columns.shape[1]
    blocked = columns.astype(jnp.float32).reshape(row_count // QB, QB, head_dim // QB, QB)
    block_peak = jnp.max(jnp.abs(blocked), axis=(1, 3)) + EPSILON
    scaled = (
        (blocked / block_peak[:, None, :, None]).reshape(row_count, head_dim).astype(jnp.bfloat16)
    )
    return (scaled, block_peak)


def shards(
    trainer_weight, hidden_new, queries, key_cache, key_scales, value_cache, value_scales, lengths
):
    replicas = lax.axis_size("replica")
    tensors = lax.axis_size("tensor")
    head_dim = key_cache.shape[3]
    stacked = lax.all_gather(trainer_weight, "replica", axis=0, tiled=True)
    regrouped = lax.all_to_all(stacked, "tensor", split_axis=1, concat_axis=0, tiled=True)
    shard_rows = trainer_weight.shape[0]
    regrouped = regrouped.reshape(tensors, replicas, shard_rows, head_dim).transpose(1, 0, 2, 3)
    synced, block_peak = quantize(regrouped.reshape(tensors * replicas * shard_rows, head_dim))
    pair_side = lax.axis_index("tensor") % 2
    upper_half = pair_side == 1
    rows_here = hidden_new.shape[0]
    blocks_r = hidden_new.shape[1] // QB
    partial_value = jnp.einsum(
        "rbi,bic->rbc",
        hidden_new.reshape(rows_here, blocks_r, QB),
        synced.reshape(blocks_r, QB, head_dim),
        preferred_element_type=jnp.float32,
    )
    column_scales = jnp.repeat(block_peak, QB, axis=1)
    projected = jnp.sum(partial_value * column_scales[None], axis=1)
    angles = lengths.astype(jnp.float32)[:, None] * frequencies(head_dim)
    rotated = rotate(projected, angles)
    own_entry = jnp.where(upper_half, projected, rotated).astype(jnp.bfloat16)
    other_entry = swapped(own_entry, "tensor", 0)
    key_fresh = jnp.where(upper_half, other_entry, own_entry)
    value_fresh = jnp.where(upper_half, own_entry, other_entry).astype(jnp.float32)
    partner_queries = swapped(queries, "tensor", 0)
    ordered = jnp.where(
        upper_half,
        jnp.concatenate([partner_queries, queries], axis=1),
        jnp.concatenate([queries, partner_queries], axis=1),
    )
    query_plain = ordered.reshape(rows_here, GROUP, head_dim)
    query_rows = query_plain.astype(jnp.float32)
    split_at = GROUP // 2
    head_number = jnp.arange(GROUP, dtype=jnp.int32)
    fresh_here = jnp.where(upper_half, head_number >= split_at, head_number < split_at)
    ctx_half = key_cache.shape[2]
    position = pair_side * ctx_half + jnp.arange(ctx_half, dtype=jnp.int32)
    live_mask = (position[None, :] < lengths[:, None]).astype(jnp.float32)
    root = math.sqrt(head_dim)
    key_rows = key_cache[:, 0].astype(jnp.float32) * key_scales[:, 0, :, None]
    value_rows = value_cache[:, 0].astype(jnp.float32) * value_scales[:, 0, :, None]
    scores = (
        jnp.einsum("rjd,rpd->rjp", query_rows, key_rows, precision=lax.Precision.HIGHEST) / root
    )
    scores = jnp.where(live_mask[:, None, :] > 0.5, scores, MASKED)
    fresh_score = (
        jnp.einsum("rjd,rd->rj", query_plain, key_fresh, preferred_element_type=jnp.float32) / root
    )
    row_peak = jnp.maximum(
        jnp.max(scores, axis=-1), jnp.where(fresh_here[None, :], fresh_score, MASKED)
    )
    weights = jnp.exp(scores - row_peak[..., None]) * live_mask[:, None, :]
    fresh_weight = jnp.where(fresh_here[None, :], jnp.exp(fresh_score - row_peak), 0.0)
    weight_sum = jnp.sum(weights, axis=-1) + fresh_weight
    weighted = jnp.einsum("rjp,rpd->rjd", weights, value_rows, precision=lax.Precision.HIGHEST)
    weighted = weighted + fresh_weight[..., None] * value_fresh[:, None, :]
    keep_peak = jnp.where(upper_half, row_peak[:, split_at:], row_peak[:, :split_at])
    keep_sum = jnp.where(upper_half, weight_sum[:, split_at:], weight_sum[:, :split_at])
    keep_weighted = jnp.where(upper_half, weighted[:, split_at:], weighted[:, :split_at])
    send_peak = jnp.where(upper_half, row_peak[:, :split_at], row_peak[:, split_at:])
    send_sum = jnp.where(upper_half, weight_sum[:, :split_at], weight_sum[:, split_at:])
    send_weighted = jnp.where(upper_half, weighted[:, :split_at], weighted[:, split_at:])
    peer_peak, peer_sum, peer_weighted = swapped((send_peak, send_sum, send_weighted), "tensor", 0)
    joint_peak = jnp.maximum(keep_peak, peer_peak)
    keep_factor = jnp.exp(keep_peak - joint_peak)
    peer_factor = jnp.exp(peer_peak - joint_peak)
    denominator = keep_sum * keep_factor + peer_sum * peer_factor
    numerator = keep_weighted * keep_factor[..., None] + peer_weighted * peer_factor[..., None]
    attended = (
        (numerator / denominator[..., None])
        .reshape(rows_here, split_at * head_dim)
        .astype(jnp.bfloat16)
    )
    return (synced, block_peak, attended)


def solution(mesh):
    placed = (
        P(("replica", "tensor"), None),
        P("replica", None),
        P("replica", "tensor"),
        P("replica", "tensor", None, None),
        P("replica", "tensor", None),
        P("replica", "tensor", None, None),
        P("replica", "tensor", None),
        P("replica"),
    )
    return jax.shard_map(
        shards,
        mesh=mesh,
        in_specs=placed,
        out_specs=(P(None, "tensor"), P(None, "tensor"), P("replica", "tensor")),
        check_vma=False,
    )
```

profile of v0, /device:TPU:66, one launch (start us, length us, event | category | flops | bytes accessed | tf_op | source)
XLA Modules:
  0.0 195.1 jit_solution(13830115411821158979)
XLA Ops:
  7.2 0.7 all-gather.3.cloned.1.call-update
  7.9 100.4 %all-gather.3.cloned.1.call-done = bf16[32,10,2048]{2,1,0:T(8,128)(2,1)} async-done(((bf16[1,10,2048]{2,1,0:T(8,128)(2,1)}), bf16[32,10,2048]{2,1,0:T(8,128)(2,1)}) %all-gather.3.cloned.1.call-update) | async-done | bytes 1310736 | tf_op jit(solution)/shard_map/all_gather | solution.py:53
  108.3 2.8 %all_to_all.10 = bf16[320,16,128]{2,1,0:T(8,128)(2,1)S(1)} reshape(bf16[32,10,2048]{2,1,0:T(8,128)(2,1)} %all-gather.3.cloned.1.call-done) | data formatting | bytes 2621440 | tf_op jit(solution)/shard_map/all_to_all | solution.py:54
  111.2 1.4 copy.16
  112.6 6.4 %all-to-all-start = ((bf16[320,16,128]{2,0,1:T(8,128)(2,1)}), bf16[320,16,128]{2,0,1:T(8,128)(2,1)S(1)}, u32[]{:S(2)}, u32[]{:S(2)}) async-start(bf16[320,16,128]{2,0,1:T(8,128)(2,1)} %copy.16), calls=%async_computation | async-start | bytes 2621440 | tf_op jit(solution)/shard_map/all_to_all | solution.py:54
  118.9 2.5 %collective-permute-start = (bf16[16,512]{1,0:T(8,128)(2,1)S(1)}, bf16[16,512]{1,0:T(8,128)(2,1)S(1)}, u32[]{:S(2)}, u32[]{:S(2)}) collective-permute-start(bf16[16,512]{1,0:T(8,128)(2,1)S(1)} %copy-done.4), channel_id=1, source_target_pairs={{0,1},{1,0},{2,3},{3,2},{4,5},{5,4},{6,7},{7,6},{8,9},{9,8},{10,11... | collective-permute-start | bytes 49160 | tf_op jit(solution)/shard_map/ppermute | solution.py:18
  121.6 4.3 %collective-permute-done = bf16[16,512]{1,0:T(8,128)(2,1)S(1)} collective-permute-done((bf16[16,512]{1,0:T(8,128)(2,1)S(1)}, bf16[16,512]{1,0:T(8,128)(2,1)S(1)}, u32[]{:S(2)}, u32[]{:S(2)}) %collective-permute-start) | collective-permute-done | bytes 16416 | tf_op jit(solution)/shard_map/ppermute | solution.py:18
  125.9 1.1 fusion.32
  127.0 22.3 %all-to-all-done = bf16[320,16,128]{2,0,1:T(8,128)(2,1)S(1)} async-done(((bf16[320,16,128]{2,0,1:T(8,128)(2,1)}), bf16[320,16,128]{2,0,1:T(8,128)(2,1)S(1)}, u32[]{:S(2)}, u32[]{:S(2)}) %all-to-all-start) | async-done | bytes 1310752 | tf_op jit(solution)/shard_map/all_to_all | solution.py:54
  149.3 0.8 copy_convert_fusion
  150.1 3.1 %copy.18 = f32[32,16,10,128]{3,2,1,0:T(8,128)} copy(f32[32,16,10,128]{3,1,2,0:T(8,128)S(1)} %bitcast.41) | data formatting | bytes 5242880 | tf_op jit(solution)/shard_map/convert_element_type | solution.py:39
  153.2 4.5 %reshape.149 = f32[40,128,128]{2,1,0:T(8,128)} reshape(f32[32,16,10,128]{3,2,1,0:T(8,128)} %copy.18) | data formatting | bytes 5242880 | tf_op jit(solution)/shard_map/convert_element_type | solution.py:39
  157.7 4.5 %reshape.148 = f32[5120,128]{1,0:T(8,128)} reshape(f32[32,16,10,128]{3,2,1,0:T(8,128)} %copy.18) | data formatting | bytes 5242880 | tf_op jit(solution)/shard_map/convert_element_type | solution.py:39
  162.2 1.0 abs_reduce_fusion
  164.0 0.5 fusion.28
  164.6 2.4 %fusion.2 = f32[128,16]{0,1:T(8,128)S(1)} fusion(f32[40,128,128]{2,1,0:T(8,128)} %reshape.149, f32[40]{0:T(128)S(1)} %get-tuple-element.15, bf16[16,5120]{1,0:T(8,128)(2,1)S(1)} %copy-done), kind=kOutput, calls=%fused_computation.6 | convolution fusion | flops 22444032 | bytes 2793632 | tf_op jit(solution)/shard_map/rbi,bic->rbc/dot_general | solution.py:62
  167.3 3.8 %collective-permute-start.1 = (bf16[16,128]{1,0:T(8,128)(2,1)S(1)}, bf16[16,128]{1,0:T(8,128)(2,1)S(1)}, u32[]{:S(2)}, u32[]{:S(2)}) collective-permute-start(bf16[16,128]{1,0:T(8,128)(2,1)S(1)} %fusion.23), channel_id=1, source_target_pairs={{0,1},{1,0},{2,3},{3,2},{4,5},{5,4},{6,7},{7,6},{8,9},{9,8},{10,11... | collective-permute-start | bytes 12296 | tf_op jit(solution)/shard_map/ppermute | solution.py:18
  171.1 3.0 %divide_convert_fusion.1 = bf16[5120,128]{1,0:T(8,128)(2,1)} fusion(f32[5120,128]{1,0:T(8,128)S(1)} %copy-done.1, f32[5120]{0:T(1024)S(1)} %broadcast_bitcast_fusion), kind=kLoop, calls=%fused_computation.2 | loop fusion | flops 1310720 | bytes 3952640 | tf_op jit(solution)/shard_map/convert_element_type | solution.py:42
  174.6 2.4 %collective-permute-start.4 = (f32[16,4]{1,0:T(8,128)S(1)}, f32[16,4]{1,0:T(8,128)S(1)}, u32[]{:S(2)}, u32[]{:S(2)}) collective-permute-start(f32[16,4]{1,0:T(8,128)S(1)} %slice_select_fusion.1), channel_id=1, source_target_pairs={{0,1},{1,0},{2,3},{3,2},{4,5},{5,4},{6,7},{7,6},{8,9},{9,8},{10,11... | collective-permute-start | bytes 776 | tf_op jit(solution)/shard_map/ppermute | solution.py:18
  177.1 3.4 %collective-permute-start.2 = (f32[16,4]{1,0:T(8,128)S(1)}, f32[16,4]{1,0:T(8,128)S(1)}, u32[]{:S(2)}, u32[]{:S(2)}) collective-permute-start(f32[16,4]{1,0:T(8,128)S(1)} %slice_select_fusion.2), channel_id=1, source_target_pairs={{0,1},{1,0},{2,3},{3,2},{4,5},{5,4},{6,7},{7,6},{8,9},{9,8},{10,11... | collective-permute-start | bytes 776 | tf_op jit(solution)/shard_map/ppermute | solution.py:18
  180.5 1.2 multiply_add_fusion
  181.7 2.4 %collective-permute-start.3 = (f32[16,4,128]{2,1,0:T(4,128)S(1)}, f32[16,4,128]{2,1,0:T(4,128)S(1)}, u32[]{:S(2)}, u32[]{:S(2)}) collective-permute-start(f32[16,4,128]{2,1,0:T(4,128)S(1)} %slice_select_fusion), channel_id=1, source_target_pairs={{0,1},{1,0},{2,3},{3,2},{4,5},{5,4},{6,7},{7,6},{8,9},{9,8},{10,11... | collective-permute-start | bytes 98312 | tf_op jit(solution)/shard_map/ppermute | solution.py:18
  184.2 3.3 %collective-permute-done.3 = f32[16,4,128]{2,1,0:T(4,128)S(1)} collective-permute-done((f32[16,4,128]{2,1,0:T(4,128)S(1)}, f32[16,4,128]{2,1,0:T(4,128)S(1)}, u32[]{:S(2)}, u32[]{:S(2)}) %collective-permute-start.3) | collective-permute-done | bytes 32800 | tf_op jit(solution)/shard_map/ppermute | solution.py:18
  187.6 0.6 copy.37
  (45 shorter events, 2.0 us)
Async XLA Ops:
  7.2 157.4 %copy-start = (bf16[16,5120]{1,0:T(8,128)(2,1)S(1)}, bf16[16,5120]{1,0:T(8,128)(2,1)}, u32[]{:S(2)}) copy-start(bf16[16,5120]{1,0:T(8,128)(2,1)} %param.9) | copy-start | bytes 491524
  7.2 101.1 %all-gather.3.cloned.1.call-start = ((), (), s32[]{:S(2)}) async-start(), calls=%async_computation.1 | async-start | bytes 2162688 | tf_op jit(solution)/shard_map/all_gather | solution.py:53
  111.1 7.8 %copy-start.4 = (bf16[16,512]{1,0:T(8,128)(2,1)S(1)}, bf16[16,512]{1,0:T(8,128)(2,1)}, u32[]{:S(2)}) copy-start(bf16[16,512]{1,0:T(8,128)(2,1)} %param.10) | copy-start | bytes 49156
  111.1 10.3 %copy-start.7 = (s32[16]{0:T(128)S(1)}, s32[16]{0:T(128)}, u32[]{:S(2)}) copy-start(s32[16]{0:T(128)} %param.15) | copy-start | bytes 196
  111.2 14.7 %copy-start.3 = (s32[16,1,128,128]{3,2,1,0:T(8,128)S(1)}, s32[16,1,128,128]{3,2,1,0:T(8,128)}, u32[]{:S(2)}) copy-start(s32[16,1,128,128]{3,2,1,0:T(8,128)} %param.11) | copy-start | bytes 3145732
  111.2 14.7 %copy-start.5 = (f32[16,1,128]{2,1,0:T(1,128)S(1)}, f32[16,1,128]{2,1,0:T(1,128)}, u32[]{:S(2)}) copy-start(f32[16,1,128]{2,1,0:T(1,128)} %param.12) | copy-start | bytes 24580
  112.6 36.7 %all-to-all-start = ((bf16[320,16,128]{2,0,1:T(8,128)(2,1)}), bf16[320,16,128]{2,0,1:T(8,128)(2,1)S(1)}, u32[]{:S(2)}, u32[]{:S(2)}) async-start(bf16[320,16,128]{2,0,1:T(8,128)(2,1)} %copy.16), calls=%async_computation | async-start | bytes 2621440 | tf_op jit(solution)/shard_map/all_to_all | solution.py:54
  118.9 6.9 %collective-permute-start = (bf16[16,512]{1,0:T(8,128)(2,1)S(1)}, bf16[16,512]{1,0:T(8,128)(2,1)S(1)}, u32[]{:S(2)}, u32[]{:S(2)}) collective-permute-start(bf16[16,512]{1,0:T(8,128)(2,1)S(1)} %copy-done.4), channel_id=1, source_target_pairs={{0,1},{1,0},{2,3},{3,2},{4,5},{5,4},{6,7},{7,6},{8,9},{9,8},{10,11... | collective-permute-start | bytes 49160 | tf_op jit(solution)/shard_map/ppermute | solution.py:18
  164.6 6.5 %copy-start.1 = (f32[5120,128]{1,0:T(8,128)S(1)}, f32[5120,128]{1,0:T(8,128)}, u32[]{:S(2)}) copy-start(f32[5120,128]{1,0:T(8,128)} %reshape.148) | copy-start | bytes 7864324
  167.0 13.5 %copy-start.2 = (s32[16,1,128,128]{3,2,1,0:T(8,128)S(1)}, s32[16,1,128,128]{3,2,1,0:T(8,128)}, u32[]{:S(2)}) copy-start(s32[16,1,128,128]{3,2,1,0:T(8,128)} %param.13) | copy-start | bytes 3145732
  167.0 13.5 %copy-start.6 = (f32[16,1,128]{2,1,0:T(1,128)S(1)}, f32[16,1,128]{2,1,0:T(1,128)}, u32[]{:S(2)}) copy-start(f32[16,1,128]{2,1,0:T(1,128)} %param.14) | copy-start | bytes 24580
  167.3 6.9 %collective-permute-start.1 = (bf16[16,128]{1,0:T(8,128)(2,1)S(1)}, bf16[16,128]{1,0:T(8,128)(2,1)S(1)}, u32[]{:S(2)}, u32[]{:S(2)}) collective-permute-start(bf16[16,128]{1,0:T(8,128)(2,1)S(1)} %fusion.23), channel_id=1, source_target_pairs={{0,1},{1,0},{2,3},{3,2},{4,5},{5,4},{6,7},{7,6},{8,9},{9,8},{10,11... | collective-permute-start | bytes 12296 | tf_op jit(solution)/shard_map/ppermute | solution.py:18
  174.6 9.5 %collective-permute-start.4 = (f32[16,4]{1,0:T(8,128)S(1)}, f32[16,4]{1,0:T(8,128)S(1)}, u32[]{:S(2)}, u32[]{:S(2)}) collective-permute-start(f32[16,4]{1,0:T(8,128)S(1)} %slice_select_fusion.1), channel_id=1, source_target_pairs={{0,1},{1,0},{2,3},{3,2},{4,5},{5,4},{6,7},{7,6},{8,9},{9,8},{10,11... | collective-permute-start | bytes 776 | tf_op jit(solution)/shard_map/ppermute | solution.py:18
  177.1 7.1 %collective-permute-start.2 = (f32[16,4]{1,0:T(8,128)S(1)}, f32[16,4]{1,0:T(8,128)S(1)}, u32[]{:S(2)}, u32[]{:S(2)}) collective-permute-start(f32[16,4]{1,0:T(8,128)S(1)} %slice_select_fusion.2), channel_id=1, source_target_pairs={{0,1},{1,0},{2,3},{3,2},{4,5},{5,4},{6,7},{7,6},{8,9},{9,8},{10,11... | collective-permute-start | bytes 776 | tf_op jit(solution)/shard_map/ppermute | solution.py:18
  181.7 5.8 %collective-permute-start.3 = (f32[16,4,128]{2,1,0:T(4,128)S(1)}, f32[16,4,128]{2,1,0:T(4,128)S(1)}, u32[]{:S(2)}, u32[]{:S(2)}) collective-permute-start(f32[16,4,128]{2,1,0:T(4,128)S(1)} %slice_select_fusion), channel_id=1, source_target_pairs={{0,1},{1,0},{2,3},{3,2},{4,5},{5,4},{6,7},{7,6},{8,9},{9,8},{10,11... | collective-permute-start | bytes 98312 | tf_op jit(solution)/shard_map/ppermute | solution.py:18
Sparse Core Ops, SparseCore 0:
  11.4 96.9 all-gather.2
where the time goes:
time: 196 us; the launch traced here: 195 us
  waiting for transfers between devices  131 us (67%)
  starting transfers between devices  20.9 us (11%)
  local copies, waits for them, and re-layouts  17.8 us (9%)
  between operations  14.3 us (7%)
  other arithmetic  6.32 us (3%)
  matrix products  4.84 us (2%)
    all_gather x1, waiting for transfers between devices, shards(): stacked = lax.all_gather(trainer_weight, 'replica', axis=0, tiled=True)  100 us
    all_to_all x1, waiting for transfers between devices, shards(): lax.all_to_all(stacked, 'tensor', split_axis=1, concat_axis=0, tiled=True)  22.3 us
    ppermute x5, starting transfers between devices, swapped(): lax.ppermute(array, axis, [(i, i ^ 1 << apart) for i in range(lax.axis_si...  14.5 us
    convert_element_type x3, local copies, waits for them, and re-layouts, quantize(): columns.astype(jnp.float32).reshape(row_count // QB, QB, head_dim // QB, QB)  12.1 us
    ppermute x5, waiting for transfers between devices, swapped(): lax.ppermute(array, axis, [(i, i ^ 1 << apart) for i in range(lax.axis_si...  7.52 us
    all_to_all x1, starting transfers between devices, shards(): lax.all_to_all(stacked, 'tensor', split_axis=1, concat_axis=0, tiled=True)  6.36 us
    all_to_all x2, local copies, waits for them, and re-layouts, shards(): lax.all_to_all(stacked, 'tensor', split_axis=1, concat_axis=0, tiled=True)  4.21 us
  transfers between devices with their start and end apart: 7, of which 4 were waited for; matrix products, arithmetic and copies ran while one was open for 3% of the time, Pallas kernels for 0%

commit v1 on v0

v1 whole, which is shorter than its diff:
```python
import math

import jax
import jax.numpy as jnp
from jax import lax
from jax.experimental import pallas as pl
from jax.experimental.pallas import tpu as pltpu
from jax.sharding import PartitionSpec as P

HEADS = 4
QB = 128
EPSILON = 1e-06
ROPE_BASE = 1000000.0
MASKED = -1e30
MESH = pl.DeviceIdType.MESH

NY = 8
PLANE = 32
TENSORS = 16


def kernel(
    w_hbm, hid_hbm, q_hbm, kc_hbm, ks_hbm, vc_hbm, vs_hbm, len_hbm,
    synced_out, scale_out, att_out,
    w_v, hid_v, q_v, pq_v, kc_v, ks_v, vc_v, vs_v, len_s,
    stage, landed, packed, gathered, scale_v,
    qs, osc, mlsc, psend, precv, esend, erecv,
    load_sem, a_send, a_recv, ring_send, ring_recv, sib_send, sib_recv,
    pair_send, pair_recv,
):
    rep = lax.axis_index("replica")
    ten = lax.axis_index("tensor")
    y = rep // 4
    zhi = (rep // 2) % 2
    core = rep % 2
    me = zhi * TENSORS + ten
    half = ten % 2

    def replica_of(yy, zz, cc):
        return (yy * 2 + zz) * 2 + cc

    def plane_id(s):
        return {"replica": replica_of(y, s // TENSORS, core), "tensor": s % TENSORS}

    up = (y + 1) % NY
    down = (y + NY - 1) % NY
    up_id = {"replica": replica_of(up, zhi, core), "tensor": ten}
    down_id = {"replica": replica_of(down, zhi, core), "tensor": ten}
    sib_id = {"replica": replica_of(y, zhi, 1 - core), "tensor": ten}
    pair_id = {"replica": rep, "tensor": ten + 1 - 2 * half}

    barrier = pltpu.get_barrier_semaphore()

    def greet(j, carry):
        s = me ^ j
        pl.semaphore_signal(barrier, inc=1, device_id=plane_id(s), device_id_type=MESH)
        return carry

    lax.fori_loop(1, PLANE, greet, 0)
    for other in (up_id, down_id, sib_id):
        pl.semaphore_signal(barrier, inc=1, device_id=other, device_id_type=MESH)

    loads = []
    for i, (src, dst) in enumerate(
        (
            (w_hbm, w_v), (q_hbm, q_v), (kc_hbm, kc_v), (ks_hbm, ks_v), (len_hbm, len_s),
            (vc_hbm, vc_v), (vs_hbm, vs_v), (hid_hbm, hid_v),
        )
    ):
        copy = pltpu.make_async_copy(src, dst, load_sem.at[i])
        copy.start()
        loads.append(copy)
    load_w, load_q, load_kc, load_ks, load_len, load_vc, load_vs, load_hid = loads

    load_w.wait()
    for t in range(TENSORS):
        stage[t] = w_v[:, t * QB:(t + 1) * QB]
    load_q.wait()
    pl.semaphore_wait(barrier, PLANE - 1 + 3)

    def pair_copy(i, src, dst):
        return pltpu.make_async_remote_copy(
            src_ref=src, dst_ref=dst, send_sem=pair_send.at[i], recv_sem=pair_recv.at[i],
            device_id=pair_id, device_id_type=MESH,
        )

    query_copy = pair_copy(0, q_v, pq_v)
    query_copy.start()

    def block_copy(j):
        s = me ^ j
        return pltpu.make_async_remote_copy(
            src_ref=stage.at[s % TENSORS], dst_ref=landed.at[me],
            send_sem=a_send.at[j], recv_sem=a_recv.at[j],
            device_id=plane_id(s), device_id_type=MESH,
        )

    def send_block(i, carry):
        block_copy(PLANE - 1 - i).start()
        return carry

    lax.fori_loop(0, PLANE - 1, send_block, 0)
    landed[me] = stage[ten]

    root = math.sqrt(QB)
    load_len.wait()
    load_kc.wait()
    load_ks.wait()
    for h in range(HEADS):
        qs[pl.ds(h, 16, stride=8), :] = q_v[:, h * QB:(h + 1) * QB].astype(jnp.float32)
    query_copy.wait_recv()
    for h in range(HEADS):
        qs[pl.ds(HEADS + h, 16, stride=8), :] = pq_v[:, h * QB:(h + 1) * QB].astype(jnp.float32)
    position = lax.broadcasted_iota(jnp.int32, (8, QB), 1) + half * QB
    lane = lax.broadcasted_iota(jnp.int32, (8, QB), 1)
    load_vc.wait()
    load_vs.wait()
    for r in range(16):
        q_r = qs[pl.ds(r * 8, 8), :].astype(jnp.bfloat16)
        k_r = kc_v[r, 0].astype(jnp.float32).astype(jnp.bfloat16)
        score = lax.dot_general(
            q_r, k_r, (((1,), (1,)), ((), ())), preferred_element_type=jnp.float32
        )
        score = score * (ks_v[r] * (1.0 / root))
        live = position < len_s[r]
        score = jnp.where(live, score, MASKED)
        peak = jnp.max(score, axis=1, keepdims=True)
        weight = jnp.where(live, jnp.exp(score - peak), 0.0)
        total = jnp.sum(weight, axis=1, keepdims=True)
        weight = weight * vs_v[r]
        high = weight.astype(jnp.bfloat16).astype(jnp.float32)
        both = jnp.concatenate([high, weight - high], axis=0).astype(jnp.bfloat16)
        v_r = vc_v[r, 0].astype(jnp.float32).astype(jnp.bfloat16)
        out = jnp.dot(both, v_r, preferred_element_type=jnp.float32)
        osc[pl.ds(r * 8, 8), :] = out[:8] + out[8:]
        mlsc[pl.ds(r * 8, 8), :] = jnp.where(lane < 64, peak, total)

    lane16 = lax.broadcasted_iota(jnp.int32, (16, QB), 1)
    small = jnp.zeros((16, QB), jnp.float32)
    for h in range(HEADS):
        psend[h] = osc[pl.ds(HEADS + h, 16, stride=8), :]
        ml = mlsc[pl.ds(HEADS + h, 16, stride=8), :]
        here = lane16 // 32 == h
        first = (lane16 // 16) % 2 == 0
        small = jnp.where(here, jnp.where(first, ml[:, 0:1], ml[:, 64:65]), small)
    psend[HEADS] = small
    partial_copy = pair_copy(1, psend, precv)
    partial_copy.start()

    row16 = lax.broadcasted_iota(jnp.int32, (16, QB), 0)
    length = jnp.zeros((16, QB), jnp.float32)
    for r in range(16):
        length = jnp.where(row16 == r, len_s[r].astype(jnp.float32), length)
    freq_index = (lane16 % 64).astype(jnp.float32)
    angle = length * jnp.exp(freq_index * (-math.log(ROPE_BASE) / 64.0))
    cosine = jnp.cos(angle)
    sine = jnp.where(lane16 < 64, -jnp.sin(angle), jnp.sin(angle))

    def rows_of(yy, zz, cc):
        return gathered.at[pl.ds(pl.multiple_of(replica_of(yy, zz, cc) * 160, 160), 160), :]

    def ring_copy(d, k, z):
        origin = (y + NY - k) % NY if d == 0 else (y + k) % NY
        ref = rows_of(origin, z, core)
        return pltpu.make_async_remote_copy(
            src_ref=ref, dst_ref=ref,
            send_sem=ring_send.at[d, k, z], recv_sem=ring_recv.at[d, k, z],
            device_id=up_id if d == 0 else down_id, device_id_type=MESH,
        )

    def sib_copy(i, origin, z):
        ref = rows_of(origin, z, core)
        return pltpu.make_async_remote_copy(
            src_ref=ref, dst_ref=ref, send_sem=sib_send.at[i, z], recv_sem=sib_recv.at[i, z],
            device_id=sib_id, device_id_type=MESH,
        )

    sends = []

    def launch(copy):
        copy.start()
        sends.append(copy)

    def wait_block(j, carry):
        block_copy(j).wait_recv()
        return carry

    lax.fori_loop(1, PLANE, wait_block, 0)
    for z in range(2):
        for t in range(TENSORS):
            packed[pl.ds((z * TENSORS + t) * 10, 10), :] = landed[z * TENSORS + t].astype(jnp.float32)
        gathered[pl.ds(pl.multiple_of(replica_of(y, z, core) * 160, 160), 160), :] = packed[
            pl.ds(z * 160, 160), :
        ].astype(jnp.bfloat16)
        launch(ring_copy(0, 0, z))
        launch(ring_copy(1, 0, z))
        launch(sib_copy(0, y, z))

    load_hid.wait()

    def process(i, origin, projected):
        for z in range(2):
            sib_copy(i, origin, z).wait_recv()
        base = pl.multiple_of(origin * 640, 640)
        for b in range(5):
            x = gathered[pl.ds(pl.multiple_of(base + b * QB, QB), QB), :].astype(jnp.float32)
            scale = jnp.max(jnp.abs(x), axis=(0, 1), keepdims=True) + EPSILON
            q = (x * (1.0 / scale)).astype(jnp.bfloat16)
            synced_out[pl.ds(pl.multiple_of(base + b * QB, QB), QB), :] = q
            h = hid_v[:, pl.ds(pl.multiple_of(base + b * QB, QB), QB)]
            part = jnp.dot(h, q, preferred_element_type=jnp.float32)
            projected = projected + part * scale
            scale_v[pl.ds(origin * 5 + b, 1), :] = jnp.broadcast_to(scale, (1, QB))
        return projected

    def forward(d, k, z):
        ring_copy(d, k, z).wait_recv()
        origin = (y + NY - k - 1) % NY if d == 0 else (y + k + 1) % NY
        if k < 2 or (k == 2 and z == d):
            launch(ring_copy(d, k + 1, z))
        launch(sib_copy(origin_index(d, k), origin, z))

    def origin_index(d, k):
        return 7 if k == 3 else 1 + 2 * k + d

    projected = jnp.zeros((16, QB), jnp.float32)
    order = (0, 1)
    waiting = [(0, y)]
    for k in range(3):
        for z in range(2):
            for d in order:
                forward(d, k, z if d == 0 else 1 - z)
            if waiting:
                projected = process(*waiting.pop(0), projected)
        waiting += [(origin_index(0, k), (y + NY - k - 1) % NY), (origin_index(1, k), (y + k + 1) % NY)]
    for d in order:
        forward(d, 3, d)
    waiting.append((7, (y + 4) % NY))

    for item in waiting[:-1]:
        projected = process(*item, projected)
    partial_copy.wait_recv()
    merged = []
    for h in range(HEADS):
        own = osc[pl.ds(h, 16, stride=8), :]
        ml = mlsc[pl.ds(h, 16, stride=8), :]
        own_peak, own_total = ml[:, 0:1], ml[:, 64:65]
        peer_peak = precv[HEADS, :, 32 * h:32 * h + 1]
        peer_total = precv[HEADS, :, 32 * h + 16:32 * h + 17]
        joint = jnp.maximum(own_peak, peer_peak)
        own_factor = jnp.exp(own_peak - joint)
        peer_factor = jnp.exp(peer_peak - joint)
        merged.append(
            (
                joint,
                own_total * own_factor + peer_total * peer_factor,
                own * own_factor + precv[h] * peer_factor,
            )
        )
    projected = process(*waiting[-1], projected)

    rotated = projected * cosine + pltpu.roll(projected, 64, 1) * sine
    esend[...] = jnp.where(half == 1, projected, rotated).astype(jnp.bfloat16)
    entry_copy = pair_copy(2, esend, erecv)
    entry_copy.start()
    scale_out[...] = scale_v[:, 0:1]
    for copy in sends:
        copy.wait_send()
    query_copy.wait_send()
    partial_copy.wait_send()

    def drain(j, carry):
        block_copy(j).wait_send()
        return carry

    lax.fori_loop(1, PLANE, drain, 0)
    entry_copy.wait()
    own = esend[...].astype(jnp.float32)
    other = erecv[...].astype(jnp.float32)
    key = jnp.where(half == 1, other, own)
    value = jnp.where(half == 1, own, other)
    for h in range(HEADS):
        joint, total, weighted = merged[h]
        q_h = q_v[:, h * QB:(h + 1) * QB].astype(jnp.float32)
        score = jnp.sum(q_h * key, axis=1, keepdims=True) / root
        peak = jnp.maximum(joint, score)
        cached = jnp.exp(joint - peak)
        fresh = jnp.exp(score - peak)
        result = (weighted * cached + fresh * value) / (total * cached + fresh)
        att_out[:, h * QB:(h + 1) * QB] = result.astype(jnp.bfloat16)


def shards(*args):
    rows, depth = args[1].shape
    bf16, f32 = jnp.bfloat16, jnp.float32
    hbm = pl.BlockSpec(memory_space=pltpu.HBM)
    vmem = pl.BlockSpec(memory_space=pltpu.VMEM)
    dma = pltpu.SemaphoreType.DMA
    return pl.pallas_call(
        kernel,
        out_shape=(
            jax.ShapeDtypeStruct((depth, QB), bf16),
            jax.ShapeDtypeStruct((depth // QB, 1), f32),
            jax.ShapeDtypeStruct((rows, HEADS * QB), bf16),
        ),
        in_specs=[hbm] * 8,
        out_specs=(vmem, vmem, vmem),
        scratch_shapes=[
            pltpu.VMEM((10, 2048), bf16),
            pltpu.VMEM((rows, depth), bf16),
            pltpu.VMEM((rows, HEADS * QB), bf16),
            pltpu.VMEM((rows, HEADS * QB), bf16),
            pltpu.VMEM((rows, 1, QB, QB), jnp.int32),
            pltpu.VMEM((rows, 1, QB), f32),
            pltpu.VMEM((rows, 1, QB, QB), jnp.int32),
            pltpu.VMEM((rows, 1, QB), f32),
            pltpu.SMEM((rows,), jnp.int32),
            pltpu.VMEM((TENSORS, 10, QB), bf16),
            pltpu.VMEM((PLANE, 10, QB), bf16),
            pltpu.VMEM((320, QB), f32),
            pltpu.VMEM((depth, QB), bf16),
            pltpu.VMEM((depth // QB, QB), f32),
            pltpu.VMEM((128, QB), f32),
            pltpu.VMEM((128, QB), f32),
            pltpu.VMEM((128, QB), f32),
            pltpu.VMEM((HEADS + 1, rows, QB), f32),
            pltpu.VMEM((HEADS + 1, rows, QB), f32),
            pltpu.VMEM((rows, QB), bf16),
            pltpu.VMEM((rows, QB), bf16),
            dma((8,)),
            dma((PLANE,)),
            dma((PLANE,)),
            dma((2, 4, 2)),
            dma((2, 4, 2)),
            dma((8, 2)),
            dma((8, 2)),
            dma((3,)),
            dma((3,)),
        ],
        compiler_params=pltpu.CompilerParams(
            collective_id=0, has_side_effects=True, vmem_limit_bytes=62000000
        ),
        cost_estimate=pl.CostEstimate(flops=60000000, bytes_accessed=6000000, transcendentals=100000),
        name="sync_decode",
    )(*args)


def solution(mesh):
    placed = (
        P(("replica", "tensor"), None),
        P("replica", None),
        P("replica", "tensor"),
        P("replica", "tensor", None, None),
        P("replica", "tensor", None),
        P("replica", "tensor", None, None),
        P("replica", "tensor", None),
        P("replica"),
    )
    return jax.shard_map(
        shards,
        mesh=mesh,
        in_specs=placed,
        out_specs=(P(None, "tensor"), P(None, "tensor"), P("replica", "tensor")),
        check_vma=False,
    )
```

time: 196 us -> 48.1 us (0.25)
  the two profiles are of different devices: /device:TPU:66 before, /device:TPU:1 now
where the time goes in v1:
time: 48.1 us; the launch traced here: 47.9 us
  Pallas kernels  42.9 us (89%)
  local copies, waits for them, and re-layouts  4.39 us (9%)
  between operations  0.64 us (1%)
    pallas_call x1, Pallas kernels, shards(): pl.pallas_call(kernel, out_shape=(jax.ShapeDtypeStruct((depth, QB), bf16)...  42.9 us
    unnamed x4, local copies, waits for them, and re-layouts  3.08 us
    pallas_call x1, local copies, waits for them, and re-layouts, shards(): pl.pallas_call(kernel, out_shape=(jax.ShapeDtypeStruct((depth, QB), bf16)...  1.31 us

profile of v1, /device:TPU:1, one launch (start us, length us, event | category | flops | bytes accessed | tf_op | source)
XLA Modules:
  0.0 47.9 jit_solution(8112197946897418950)
XLA Ops:
  0.6 42.9 %sync_decode.1 = (bf16[5120,128]{1,0:T(8,128)(2,1)}, f32[40,1]{1,0:T(8,128)}, bf16[16,512]{1,0:T(8,128)(2,1)}) custom-call(bf16[10,2048]{1,0:T(8,128)(2,1)} %w_hbm.1, bf16[16,5120]{1,0:T(8,128)(2,1)} %hid_hbm.1, bf16[16,512]{1,0:T(8,128)(2,1)} %q_hbm.1, s32[16,1,128,128]{3,2,1,0:T(8,128)} %kc_hbm.1, f32[16,1,128]{2,1,0:T(1,128)} %ks_hbm.1, ...), custom_call_target="tpu_custom_call" | custom-call | flops 60000000 | bytes 6000000 | tf_op jit(solution)/shard_map/sync_decode/pallas_call | solution.py:299
  43.5 1.3 %copy.11 = f32[40,1]{0,1:T(1,128)} copy(f32[40,1]{1,0:T(8,128)} %get-tuple-element.4) | data formatting | bytes 320 | tf_op jit(solution)/shard_map/sync_decode/pallas_call | solution.py:299
  44.8 0.0 copy-start
  44.8 2.5 %copy.14 = bf16[5120,128]{1,0:T(8,128)(2,1)} copy(bf16[5120,128]{1,0:T(8,128)(2,1)} %get-tuple-element.9) | data formatting | bytes 2621440
  47.3 0.0 copy-done
  47.3 0.6 %copy.15 = bf16[16,512]{1,0:T(8,128)(2,1)} copy(bf16[16,512]{1,0:T(8,128)(2,1)S(1)} %copy-done) | data formatting | bytes 32768
Async XLA Ops:
  44.8 2.5 %copy-start = (bf16[16,512]{1,0:T(8,128)(2,1)S(1)}, bf16[16,512]{1,0:T(8,128)(2,1)}, u32[]{:S(2)}) copy-start(bf16[16,512]{1,0:T(8,128)(2,1)} %get-tuple-element.11) | copy-start | bytes 49156

commit v2 on v1

v2 whole, which is shorter than its diff:
```python
import math

import jax
import jax.numpy as jnp
from jax import lax
from jax.experimental import pallas as pl
from jax.experimental.pallas import tpu as pltpu
from jax.sharding import PartitionSpec as P

HEADS = 4
QB = 128
EPSILON = 1e-06
ROPE_BASE = 1000000.0
MASKED = -1e30
MESH = pl.DeviceIdType.MESH

NY = 8
NX = 4
NZ = 8
ZLO = 4
TENSORS = 16
SEND_ORDER = (2, 6, 1, 7, 0, 3, 5, 4)
LAST = 7


def kernel(
    w_hbm, hid_hbm, q_hbm, kc_hbm, ks_hbm, vc_hbm, vs_hbm, len_hbm,
    synced_out, scale_out, att_out,
    w_v, hid_v, q_v, pq_v, kc_v, ks_v, vc_v, vs_v, len_s,
    stage, landed, packed, gathered, group, scale_v,
    qs, osc, mlsc, psend, precv, esend, erecv,
    load_sem, plane_send, plane_recv, ring_send, ring_recv, sib_send, sib_recv,
    pair_send, pair_recv,
):
    rep = lax.axis_index("replica")
    ten = lax.axis_index("tensor")
    y = rep // 4
    zhi = (rep // 2) % 2
    core = rep % 2
    half = ten % 2
    x = ten % NX
    z = zhi * ZLO + ten // NX

    def replica_of(yy, zz, cc):
        return (yy * 2 + zz) * 2 + cc

    def plane_id(zz, xx):
        return {"replica": replica_of(y, zz // ZLO, core), "tensor": (zz % ZLO) * NX + xx}

    def along_y(steps):
        return {"replica": replica_of((y + NY + steps) % NY, zhi, core), "tensor": ten}

    sib_id = {"replica": replica_of(y, zhi, 1 - core), "tensor": ten}
    pair_id = plane_id(z, x ^ 1)

    loads = [
        pltpu.make_async_copy(src, dst, load_sem.at[i])
        for i, (src, dst) in enumerate(
            (
                (w_hbm, w_v), (q_hbm, q_v), (kc_hbm, kc_v), (ks_hbm, ks_v), (len_hbm, len_s),
                (vc_hbm, vc_v), (vs_hbm, vs_v), (hid_hbm, hid_v),
            )
        )
    ]
    load_w, load_q, load_kc, load_ks, load_len, load_vc, load_vs, load_hid = loads
    load_w.start()
    load_q.start()

    barrier = pltpu.get_barrier_semaphore()
    peers = [
        plane_id((z + dz) % NZ, x ^ dx)
        for dz in (4, 3, 5, 2, 6, 1, 7, 0) for dx in (2, 3, 1, 0) if dz or dx
    ]
    peers += [along_y(2), along_y(-2), along_y(1), along_y(-1), sib_id]
    for other in peers:
        pl.semaphore_signal(barrier, inc=1, device_id=other, device_id_type=MESH)
    for copy in loads[2:]:
        copy.start()

    load_w.wait()
    for t in range(TENSORS):
        stage[t] = w_v[:, t * QB:(t + 1) * QB]
    load_q.wait()
    pl.semaphore_wait(barrier, len(peers))

    sends = []

    def launch(copy):
        copy.start()
        sends.append(copy)

    def pair_copy(i, src, dst):
        return pltpu.make_async_remote_copy(
            src_ref=src, dst_ref=dst, send_sem=pair_send.at[i], recv_sem=pair_recv.at[i],
            device_id=pair_id, device_id_type=MESH,
        )

    def plane_copy(j):
        to_z, to_x = (z + j // NX) % NZ, x ^ (j % NX)
        return pltpu.make_async_remote_copy(
            src_ref=stage.at[(to_z % ZLO) * NX + to_x], dst_ref=landed.at[z * NX + x],
            send_sem=plane_send.at[j], recv_sem=plane_recv.at[j],
            device_id=plane_id(to_z, to_x), device_id_type=MESH,
        )

    query_copy = pair_copy(0, q_v, pq_v)
    launch(query_copy)
    for dz in SEND_ORDER:
        for dx in (2, 3, 1, 0):
            if dz or dx:
                launch(plane_copy(dz * NX + dx))
    landed[z * NX + x] = stage[ten]

    root = math.sqrt(QB)
    load_len.wait()
    load_kc.wait()
    load_ks.wait()
    for h in range(HEADS):
        qs[pl.ds(h, 16, stride=8), :] = q_v[:, h * QB:(h + 1) * QB].astype(jnp.float32)
    query_copy.wait_recv()
    for h in range(HEADS):
        qs[pl.ds(HEADS + h, 16, stride=8), :] = pq_v[:, h * QB:(h + 1) * QB].astype(jnp.float32)
    position = lax.broadcasted_iota(jnp.int32, (8, QB), 1) + half * QB
    lane = lax.broadcasted_iota(jnp.int32, (8, QB), 1)
    load_vc.wait()
    load_vs.wait()
    for r in range(16):
        q_r = qs[pl.ds(r * 8, 8), :].astype(jnp.bfloat16)
        k_r = kc_v[r, 0].astype(jnp.float32).astype(jnp.bfloat16)
        score = lax.dot_general(
            q_r, k_r, (((1,), (1,)), ((), ())), preferred_element_type=jnp.float32
        )
        score = score * (ks_v[r] * (1.0 / root))
        live = position < len_s[r]
        score = jnp.where(live, score, MASKED)
        peak = jnp.max(score, axis=1, keepdims=True)
        weight = jnp.where(live, jnp.exp(score - peak), 0.0)
        total = jnp.sum(weight, axis=1, keepdims=True)
        weight = weight * vs_v[r]
        high = weight.astype(jnp.bfloat16).astype(jnp.float32)
        both = jnp.concatenate([high, weight - high], axis=0).astype(jnp.bfloat16)
        v_r = vc_v[r, 0].astype(jnp.float32).astype(jnp.bfloat16)
        out = jnp.dot(both, v_r, preferred_element_type=jnp.float32)
        osc[pl.ds(r * 8, 8), :] = out[:8] + out[8:]
        mlsc[pl.ds(r * 8, 8), :] = jnp.where(lane < 64, peak, total)

    lane16 = lax.broadcasted_iota(jnp.int32, (16, QB), 1)
    small = jnp.zeros((16, QB), jnp.float32)
    for h in range(HEADS):
        psend[h] = osc[pl.ds(HEADS + h, 16, stride=8), :]
        ml = mlsc[pl.ds(HEADS + h, 16, stride=8), :]
        here = lane16 // 32 == h
        first = (lane16 // 16) % 2 == 0
        small = jnp.where(here, jnp.where(first, ml[:, 0:1], ml[:, 64:65]), small)
    psend[HEADS] = small
    partial_copy = pair_copy(1, psend, precv)
    launch(partial_copy)

    near = z // 2
    odd = z % 2
    pairs = (near, (near + 3 + 2 * odd) % 4, (near + 1 + 2 * odd) % 4, (near + 2) % 4)

    def chunk(yy, cc, piece):
        base = (yy * 2 + cc) * 320 + (160 if piece == 1 else 0)
        return pl.ds(pl.multiple_of(base, 160), 320 if piece is None else 160)

    def origin_of(d, k):
        return (y + NY - k) % NY if d == 0 else (y + k) % NY

    def ring_copy(piece, d, k):
        leg = 2 if k % 2 == 0 else 1
        ref = gathered.at[chunk(origin_of(d, k - leg), core, piece), :]
        return pltpu.make_async_remote_copy(
            src_ref=ref, dst_ref=ref,
            send_sem=ring_send.at[d, k - 1, piece], recv_sem=ring_recv.at[d, k - 1, piece],
            device_id=along_y(leg if d == 0 else -leg), device_id_type=MESH,
        )

    def arrived(piece, d, k):
        leg = 2 if k % 2 == 0 else 1
        ref = gathered.at[chunk(origin_of(d, k), core, piece), :]
        pltpu.make_async_remote_copy(
            src_ref=ref, dst_ref=ref,
            send_sem=ring_send.at[d, k - 1, piece], recv_sem=ring_recv.at[d, k - 1, piece],
            device_id=along_y(leg if d == 0 else -leg), device_id_type=MESH,
        ).wait_recv()

    def sib_copy(i, origin, piece, cc):
        ref = gathered.at[chunk(origin, cc, piece), :]
        return pltpu.make_async_remote_copy(
            src_ref=ref, dst_ref=ref, send_sem=sib_send.at[i], recv_sem=sib_recv.at[i],
            device_id=sib_id, device_id_type=MESH,
        )

    def plane_wait(dz):
        for dx in range(NX):
            plane_copy(dz * NX + dx).wait_recv()

    def start_piece(piece):
        for i in range(2):
            for side in range(2):
                for e in range(NX):
                    packed[pl.ds((2 * i + side) * 40 + e * 10, 10), :] = landed[
                        (2 * pairs[2 * piece + i] + side) * NX + e
                    ].astype(jnp.float32)
        gathered[chunk(y, core, piece), :] = packed[...].astype(jnp.bfloat16)
        for k in (2, 1):
            for d in range(2):
                launch(ring_copy(piece, d, k))

    for dx in range(1, NX):
        plane_copy(dx).wait_recv()
    for dz in (1, 7, 2 + 4 * odd):
        plane_wait(dz)
    start_piece(0)
    for dz in (6 - 4 * odd, 3, 5, 4):
        plane_wait(dz)
    start_piece(1)
    launch(sib_copy(0, y, None, core))

    row16 = lax.broadcasted_iota(jnp.int32, (16, QB), 0)
    length = jnp.zeros((16, QB), jnp.float32)
    for r in range(16):
        length = jnp.where(row16 == r, len_s[r].astype(jnp.float32), length)
    freq_index = (lane16 % 64).astype(jnp.float32)
    angle = length * jnp.exp(freq_index * (-math.log(ROPE_BASE) / 64.0))
    cosine = jnp.cos(angle)
    sine = jnp.where(lane16 < 64, -jnp.sin(angle), jnp.sin(angle))

    load_hid.wait()

    def process(i, origin, projected):
        if i == LAST:
            for piece in range(2):
                sib_copy(LAST + piece, origin, piece, 1 - core).wait_recv()
        else:
            sib_copy(i, origin, None, 1 - core).wait_recv()
        for cc in range(2):
            for q in range(4):
                to = (pairs[q] // 2) * 320 + cc * 160 + (pairs[q] % 2) * 80
                at = (origin * 2 + cc) * 320 + q * 80
                group[pl.ds(pl.multiple_of(to, 80), 80), :] = gathered[pl.ds(pl.multiple_of(at, 80), 80), :]
        base = pl.multiple_of(origin * 640, 640)
        for b in range(5):
            raw = group[pl.ds(b * QB, QB), :].astype(jnp.float32)
            scale = jnp.max(jnp.abs(raw), axis=(0, 1), keepdims=True) + EPSILON
            q = (raw * (1.0 / scale)).astype(jnp.bfloat16)
            synced_out[pl.ds(pl.multiple_of(base + b * QB, QB), QB), :] = q
            h = hid_v[:, pl.ds(pl.multiple_of(base + b * QB, QB), QB)]
            part = jnp.dot(h, q, preferred_element_type=jnp.float32)
            projected = projected + part * scale
            scale_v[pl.ds(origin * 5 + b, 1), :] = jnp.broadcast_to(scale, (1, QB))
        return projected

    def receive(piece, k):
        for d in (0, 1) if k < 4 else (1 - piece,):
            arrived(piece, d, k)
            if k == 2:
                if d == 1 - piece:
                    launch(ring_copy(piece, d, 4))
                launch(ring_copy(piece, d, 3))
        if k == 4:
            launch(sib_copy(LAST + piece, origin_of(0, 4), piece, core))

    def share(k):
        for d in range(2):
            launch(sib_copy(2 * k - 1 + d, origin_of(d, k), None, core))

    projected = jnp.zeros((16, QB), jnp.float32)
    receive(0, 2)
    receive(0, 1)
    receive(1, 2)
    share(2)
    receive(1, 1)
    share(1)
    projected = process(0, y, projected)
    receive(0, 3)
    for d in range(2):
        projected = process(3 + d, origin_of(d, 2), projected)
    receive(1, 3)
    share(3)
    for d in range(2):
        projected = process(1 + d, origin_of(d, 1), projected)
    receive(0, 4)
    receive(1, 4)
    for d in range(2):
        projected = process(5 + d, origin_of(d, 3), projected)

    partial_copy.wait_recv()
    merged = []
    for h in range(HEADS):
        own = osc[pl.ds(h, 16, stride=8), :]
        ml = mlsc[pl.ds(h, 16, stride=8), :]
        own_peak, own_total = ml[:, 0:1], ml[:, 64:65]
        peer_peak = precv[HEADS, :, 32 * h:32 * h + 1]
        peer_total = precv[HEADS, :, 32 * h + 16:32 * h + 17]
        joint = jnp.maximum(own_peak, peer_peak)
        own_factor = jnp.exp(own_peak - joint)
        peer_factor = jnp.exp(peer_peak - joint)
        merged.append(
            (
                joint,
                own_total * own_factor + peer_total * peer_factor,
                own * own_factor + precv[h] * peer_factor,
            )
        )
    projected = process(LAST, origin_of(0, 4), projected)

    rotated = projected * cosine + pltpu.roll(projected, 64, 1) * sine
    esend[...] = jnp.where(half == 1, projected, rotated).astype(jnp.bfloat16)
    entry_copy = pair_copy(2, esend, erecv)
    entry_copy.start()
    scale_out[...] = jnp.transpose(scale_v[...], (1, 0))[0:1, 0:40]
    for copy in sends:
        copy.wait_send()
    entry_copy.wait()
    own = esend[...].astype(jnp.float32)
    other = erecv[...].astype(jnp.float32)
    key = jnp.where(half == 1, other, own)
    value = jnp.where(half == 1, own, other)
    for h in range(HEADS):
        joint, total, weighted = merged[h]
        q_h = q_v[:, h * QB:(h + 1) * QB].astype(jnp.float32)
        score = jnp.sum(q_h * key, axis=1, keepdims=True) / root
        peak = jnp.maximum(joint, score)
        cached = jnp.exp(joint - peak)
        fresh = jnp.exp(score - peak)
        result = (weighted * cached + fresh * value) / (total * cached + fresh)
        att_out[:, h * QB:(h + 1) * QB] = result.astype(jnp.bfloat16)


PARTS = 4


def settle(synced, scales, attended, synced_out, scales_out, attended_out, sem):
    step = synced.shape[0] // PARTS
    legs = [(scales, scales_out), (attended, attended_out)]
    legs += [(ref.at[pl.ds(i * step, step), :], out.at[pl.ds(i * step, step), :])
             for ref, out in ((synced, synced_out),) for i in range(PARTS)]
    copies = [pltpu.make_async_copy(one, other, sem.at[i]) for i, (one, other) in enumerate(legs)]
    for copy in copies:
        copy.start()
    for copy in copies:
        copy.wait()


def shards(*args):
    rows, depth = args[1].shape
    bf16, f32 = jnp.bfloat16, jnp.float32
    hbm = pl.BlockSpec(memory_space=pltpu.HBM)
    vmem = pl.BlockSpec(memory_space=pltpu.VMEM)
    dma = pltpu.SemaphoreType.DMA
    synced, scales, attended = pl.pallas_call(
        kernel,
        out_shape=(
            pltpu.VMEM((depth, QB), bf16),
            pltpu.VMEM((1, depth // QB), f32),
            pltpu.VMEM((rows, HEADS * QB), bf16),
        ),
        in_specs=[hbm] * 8,
        out_specs=(vmem, vmem, vmem),
        scratch_shapes=[
            pltpu.VMEM((10, 2048), bf16),
            pltpu.VMEM((rows, depth), bf16),
            pltpu.VMEM((rows, HEADS * QB), bf16),
            pltpu.VMEM((rows, HEADS * QB), bf16),
            pltpu.VMEM((rows, 1, QB, QB), jnp.int32),
            pltpu.VMEM((rows, 1, QB), f32),
            pltpu.VMEM((rows, 1, QB, QB), jnp.int32),
            pltpu.VMEM((rows, 1, QB), f32),
            pltpu.SMEM((rows,), jnp.int32),
            pltpu.VMEM((TENSORS, 10, QB), bf16),
            pltpu.VMEM((NZ * NX, 10, QB), bf16),
            pltpu.VMEM((160, QB), f32),
            pltpu.VMEM((depth, QB), bf16),
            pltpu.VMEM((640, QB), bf16),
            pltpu.VMEM((128, QB), f32),
            pltpu.VMEM((128, QB), f32),
            pltpu.VMEM((128, QB), f32),
            pltpu.VMEM((128, QB), f32),
            pltpu.VMEM((HEADS + 1, rows, QB), f32),
            pltpu.VMEM((HEADS + 1, rows, QB), f32),
            pltpu.VMEM((rows, QB), bf16),
            pltpu.VMEM((rows, QB), bf16),
            dma((8,)),
            dma((NZ * NX,)),
            dma((NZ * NX,)),
            dma((2, 4, 2)),
            dma((2, 4, 2)),
            dma((9,)),
            dma((9,)),
            dma((3,)),
            dma((3,)),
        ],
        compiler_params=pltpu.CompilerParams(
            collective_id=0, has_side_effects=True, vmem_limit_bytes=62000000
        ),
        cost_estimate=pl.CostEstimate(flops=60000000, bytes_accessed=6000000, transcendentals=100000),
        name="sync_decode",
    )(*args)
    synced, scales, attended = pl.pallas_call(
        settle,
        out_shape=(
            jax.ShapeDtypeStruct((depth, QB), bf16),
            jax.ShapeDtypeStruct((1, depth // QB), f32),
            jax.ShapeDtypeStruct((rows, HEADS * QB), bf16),
        ),
        in_specs=[vmem] * 3,
        out_specs=(hbm,) * 3,
        scratch_shapes=[dma((PARTS + 2,))],
        compiler_params=pltpu.CompilerParams(vmem_limit_bytes=8 * 1024 * 1024),
        name="settle",
    )(synced, scales, attended)
    return synced, scales.reshape(depth // QB, 1), attended


def solution(mesh):
    placed = (
        P(("replica", "tensor"), None),
        P("replica", None),
        P("replica", "tensor"),
        P("replica", "tensor", None, None),
        P("replica", "tensor", None),
        P("replica", "tensor", None, None),
        P("replica", "tensor", None),
        P("replica"),
    )
    return jax.shard_map(
        shards,
        mesh=mesh,
        in_specs=placed,
        out_specs=(P(None, "tensor"), P(None, "tensor"), P("replica", "tensor")),
        check_vma=False,
    )
```

time: 48.1 us -> 41.2 us (0.86)
  local copies, waits for them, and re-layouts: 4.39 us -> 0 us
  Pallas kernels: 42.9 us -> 40.4 us
    unnamed x4 -> x0, local copies, waits for them, and re-layouts: 3.08 us -> none
    pallas_call x1 -> x2, Pallas kernels: 42.9 us -> 40.4 us  [the longest x1 39.2 us: shards(): pl.pallas_call(kernel, out_shape=(pltpu.VMEM((depth, QB), bf16), pltpu.VM...]
    pallas_call x1 -> x0, local copies, waits for them, and re-layouts: 1.31 us -> none  [shards(): pl.pallas_call(kernel, out_shape=(jax.ShapeDtypeStruct((depth, QB), bf16)...]
where the time goes in v2:
time: 41.2 us; the launch traced here: 41 us
  Pallas kernels  40.4 us (98%)
  between operations  0.64 us (2%)
    pallas_call x1, Pallas kernels, shards(): pl.pallas_call(kernel, out_shape=(pltpu.VMEM((depth, QB), bf16), pltpu.VM...  39.2 us
    pallas_call x1, Pallas kernels, shards(): pl.pallas_call(settle, out_shape=(jax.ShapeDtypeStruct((depth, QB), bf16)...  1.11 us

profile of v2, /device:TPU:1, one launch (start us, length us, event | category | flops | bytes accessed | tf_op | source)
XLA Modules:
  0.0 41.0 jit_solution(2449093940425275856)
XLA Ops:
  0.6 39.2 %sync_decode.1 = (bf16[5120,128]{1,0:T(8,128)(2,1)S(1)}, f32[1,40]{1,0:T(1,128)S(1)}, bf16[16,512]{1,0:T(8,128)(2,1)S(1)}) custom-call(bf16[10,2048]{1,0:T(8,128)(2,1)} %w_hbm.1, bf16[16,5120]{1,0:T(8,128)(2,1)} %hid_hbm.1, bf16[16,512]{1,0:T(8,128)(2,1)} %q_hbm.1, s32[16,1,128,128]{3,2,1,0:T(8,128)} %kc_hbm.1, f32[16,1,128]{2,1,0:T(1,128)} %ks_hbm.1, ...), custom_call_target="tpu_custom_call" | custom-call | flops 60000000 | bytes 6000000 | tf_op jit(solution)/shard_map/sync_decode/pallas_call | solution.py:353
  39.9 1.1 %settle.1 = (bf16[5120,128]{1,0:T(8,128)(2,1)}, f32[1,40]{1,0:T(1,128)}, bf16[16,512]{1,0:T(8,128)(2,1)}) custom-call(bf16[5120,128]{1,0:T(8,128)(2,1)S(1)} %get-tuple-element.9.synced, f32[1,40]{1,0:T(1,128)S(1)} %get-tuple-element.10.scales, bf16[16,512]{1,0:T(8,128)(2,1)S(1)} %get-tuple-element.11.attended), custom_call_target="tpu_custom_call" | custom-call | tf_op jit(solution)/shard_map/settle/pallas_call | solution.py:401

commit v3 on v2

--- a/solution.py
+++ b/solution.py
@@ -112,49 +112,56 @@
     landed[z * NX + x] = stage[ten]
 
     root = math.sqrt(QB)
-    load_len.wait()
-    load_kc.wait()
-    load_ks.wait()
-    for h in range(HEADS):
-        qs[pl.ds(h, 16, stride=8), :] = q_v[:, h * QB:(h + 1) * QB].astype(jnp.float32)
-    query_copy.wait_recv()
-    for h in range(HEADS):
-        qs[pl.ds(HEADS + h, 16, stride=8), :] = pq_v[:, h * QB:(h + 1) * QB].astype(jnp.float32)
     position = lax.broadcasted_iota(jnp.int32, (8, QB), 1) + half * QB
     lane = lax.broadcasted_iota(jnp.int32, (8, QB), 1)
-    load_vc.wait()
-    load_vs.wait()
-    for r in range(16):
-        q_r = qs[pl.ds(r * 8, 8), :].astype(jnp.bfloat16)
-        k_r = kc_v[r, 0].astype(jnp.float32).astype(jnp.bfloat16)
-        score = lax.dot_general(
-            q_r, k_r, (((1,), (1,)), ((), ())), preferred_element_type=jnp.float32
-        )
-        score = score * (ks_v[r] * (1.0 / root))
-        live = position < len_s[r]
-        score = jnp.where(live, score, MASKED)
-        peak = jnp.max(score, axis=1, keepdims=True)
-        weight = jnp.where(live, jnp.exp(score - peak), 0.0)
-        total = jnp.sum(weight, axis=1, keepdims=True)
-        weight = weight * vs_v[r]
-        high = weight.astype(jnp.bfloat16).astype(jnp.float32)
-        both = jnp.concatenate([high, weight - high], axis=0).astype(jnp.bfloat16)
-        v_r = vc_v[r, 0].astype(jnp.float32).astype(jnp.bfloat16)
-        out = jnp.dot(both, v_r, preferred_element_type=jnp.float32)
-        osc[pl.ds(r * 8, 8), :] = out[:8] + out[8:]
-        mlsc[pl.ds(r * 8, 8), :] = jnp.where(lane < 64, peak, total)
-
     lane16 = lax.broadcasted_iota(jnp.int32, (16, QB), 1)
-    small = jnp.zeros((16, QB), jnp.float32)
-    for h in range(HEADS):
-        psend[h] = osc[pl.ds(HEADS + h, 16, stride=8), :]
-        ml = mlsc[pl.ds(HEADS + h, 16, stride=8), :]
-        here = lane16 // 32 == h
-        first = (lane16 // 16) % 2 == 0
-        small = jnp.where(here, jnp.where(first, ml[:, 0:1], ml[:, 64:65]), small)
-    psend[HEADS] = small
+
+    def ready_queries():
+        load_len.wait()
+        load_kc.wait()
+        load_ks.wait()
+        for h in range(HEADS):
+            qs[pl.ds(h, 16, stride=8), :] = q_v[:, h * QB:(h + 1) * QB].astype(jnp.float32)
+        query_copy.wait_recv()
+        for h in range(HEADS):
+            qs[pl.ds(HEADS + h, 16, stride=8), :] = pq_v[:, h * QB:(h + 1) * QB].astype(jnp.float32)
+        load_vc.wait()
+        load_vs.wait()
+
+    def attend(first, last):
+        for r in range(first, last):
+            q_r = qs[pl.ds(r * 8, 8), :].astype(jnp.bfloat16)
+            k_r = kc_v[r, 0].astype(jnp.float32).astype(jnp.bfloat16)
+            score = lax.dot_general(
+                q_r, k_r, (((1,), (1,)), ((), ())), preferred_element_type=jnp.float32
+            )
+            score = score * (ks_v[r] * (1.0 / root))
+            live = position < len_s[r]
+            score = jnp.where(live, score, MASKED)
+            peak = jnp.max(score, axis=1, keepdims=True)
+            weight = jnp.where(live, jnp.exp(score - peak), 0.0)
+            total = jnp.sum(weight, axis=1, keepdims=True)
+            weight = weight * vs_v[r]
+            high = weight.astype(jnp.bfloat16).astype(jnp.float32)
+            both = jnp.concatenate([high, weight - high], axis=0).astype(jnp.bfloat16)
+            v_r = vc_v[r, 0].astype(jnp.float32).astype(jnp.bfloat16)
+            out = jnp.dot(both, v_r, preferred_element_type=jnp.float32)
+            osc[pl.ds(r * 8, 8), :] = out[:8] + out[8:]
+            mlsc[pl.ds(r * 8, 8), :] = jnp.where(lane < 64, peak, total)
+
+
     partial_copy = pair_copy(1, psend, precv)
-    launch(partial_copy)
+
+    def send_partials():
+        small = jnp.zeros((16, QB), jnp.float32)
+        for h in range(HEADS):
+            psend[h] = osc[pl.ds(HEADS + h, 16, stride=8), :]
+            ml = mlsc[pl.ds(HEADS + h, 16, stride=8), :]
+            here = lane16 // 32 == h
+            first = (lane16 // 16) % 2 == 0
+            small = jnp.where(here, jnp.where(first, ml[:, 0:1], ml[:, 64:65]), small)
+        psend[HEADS] = small
+        launch(partial_copy)
 
     near = z // 2
     odd = z % 2
@@ -217,6 +224,9 @@
         plane_wait(dz)
     start_piece(1)
     launch(sib_copy(0, y, None, core))
+    ready_queries()
+    attend(0, 16)
+    send_partials()
 
     row16 = lax.broadcasted_iota(jnp.int32, (16, QB), 0)
     length = jnp.zeros((16, QB), jnp.float32)

time: 41.2 us -> 38 us (0.922)
  Pallas kernels: 40.4 us -> 37.2 us
    pallas_call x1, Pallas kernels: 39.2 us -> 36 us  [shards(): pl.pallas_call(kernel, out_shape=(pltpu.VMEM((depth, QB), bf16), pltpu.VM...]
where the time goes in v3:
time: 38 us; the launch traced here: 37.8 us
  Pallas kernels  37.2 us (98%)
  between operations  0.64 us (2%)
    pallas_call x1, Pallas kernels, shards(): pl.pallas_call(kernel, out_shape=(pltpu.VMEM((depth, QB), bf16), pltpu.VM...  36 us
    pallas_call x1, Pallas kernels, shards(): pl.pallas_call(settle, out_shape=(jax.ShapeDtypeStruct((depth, QB), bf16)...  1.11 us

profile of v3, /device:TPU:1, one launch (start us, length us, event | category | flops | bytes accessed | tf_op | source)
XLA Modules:
  0.0 37.8 jit_solution(9860801108622455619)
XLA Ops:
  0.6 36.0 %sync_decode.1 = (bf16[5120,128]{1,0:T(8,128)(2,1)S(1)}, f32[1,40]{1,0:T(1,128)S(1)}, bf16[16,512]{1,0:T(8,128)(2,1)S(1)}) custom-call(bf16[10,2048]{1,0:T(8,128)(2,1)} %w_hbm.1, bf16[16,5120]{1,0:T(8,128)(2,1)} %hid_hbm.1, bf16[16,512]{1,0:T(8,128)(2,1)} %q_hbm.1, s32[16,1,128,128]{3,2,1,0:T(8,128)} %kc_hbm.1, f32[16,1,128]{2,1,0:T(1,128)} %ks_hbm.1, ...), custom_call_target="tpu_custom_call" | custom-call | flops 60000000 | bytes 6000000 | tf_op jit(solution)/shard_map/sync_decode/pallas_call | solution.py:363
  36.7 1.1 %settle.1 = (bf16[5120,128]{1,0:T(8,128)(2,1)}, f32[1,40]{1,0:T(1,128)}, bf16[16,512]{1,0:T(8,128)(2,1)}) custom-call(bf16[5120,128]{1,0:T(8,128)(2,1)S(1)} %get-tuple-element.9.synced, f32[1,40]{1,0:T(1,128)S(1)} %get-tuple-element.10.scales, bf16[16,512]{1,0:T(8,128)(2,1)S(1)} %get-tuple-element.11.attended), custom_call_target="tpu_custom_call" | custom-call | tf_op jit(solution)/shard_map/settle/pallas_call | solution.py:411

commit v4 on v3

--- a/solution.py
+++ b/solution.py
@@ -19,7 +19,6 @@
 NZ = 8
 ZLO = 4
 TENSORS = 16
-SEND_ORDER = (2, 6, 1, 7, 0, 3, 5, 4)
 LAST = 7
 
 
@@ -29,7 +28,7 @@
     w_v, hid_v, q_v, pq_v, kc_v, ks_v, vc_v, vs_v, len_s,
     stage, landed, packed, gathered, group, scale_v,
     qs, osc, mlsc, psend, precv, esend, erecv,
-    load_sem, plane_send, plane_recv, ring_send, ring_recv, sib_send, sib_recv,
+    merged, load_sem, plane_send, plane_recv, row_send, ring_recv, sib_recv,
     pair_send, pair_recv,
 ):
     rep = lax.axis_index("replica")
@@ -95,20 +94,24 @@
             device_id=pair_id, device_id_type=MESH,
         )
 
-    def plane_copy(j):
-        to_z, to_x = (z + j // NX) % NZ, x ^ (j % NX)
+    odd = z % 2
+    offsets = ((2 + 4 * odd, 1, 7, 0), (6 - 4 * odd, 3, 5, 4))
+
+    def plane_copy(part, dz, dx):
+        to_z, to_x = (z + dz) % NZ, x ^ dx
         return pltpu.make_async_remote_copy(
             src_ref=stage.at[(to_z % ZLO) * NX + to_x], dst_ref=landed.at[z * NX + x],
-            send_sem=plane_send.at[j], recv_sem=plane_recv.at[j],
+            send_sem=plane_send, recv_sem=plane_recv.at[part],
             device_id=plane_id(to_z, to_x), device_id_type=MESH,
         )
 
     query_copy = pair_copy(0, q_v, pq_v)
     launch(query_copy)
-    for dz in SEND_ORDER:
-        for dx in (2, 3, 1, 0):
-            if dz or dx:
-                launch(plane_copy(dz * NX + dx))
+    for part in range(2):
+        for i, dz in enumerate(offsets[part]):
+            for dx in (2, 3, 1, 0):
+                if (part, i, dx) != (0, 3, 0):
+                    plane_copy(part, dz, dx).start()
     landed[z * NX + x] = stage[ten]
 
     root = math.sqrt(QB)
@@ -164,7 +167,6 @@
         launch(partial_copy)
 
     near = z // 2
-    odd = z % 2
     pairs = (near, (near + 3 + 2 * odd) % 4, (near + 1 + 2 * odd) % 4, (near + 2) % 4)
 
     def chunk(yy, cc, piece):
@@ -179,7 +181,7 @@
         ref = gathered.at[chunk(origin_of(d, k - leg), core, piece), :]
         return pltpu.make_async_remote_copy(
             src_ref=ref, dst_ref=ref,
-            send_sem=ring_send.at[d, k - 1, piece], recv_sem=ring_recv.at[d, k - 1, piece],
+            send_sem=row_send, recv_sem=ring_recv.at[d, k - 1, piece],
             device_id=along_y(leg if d == 0 else -leg), device_id_type=MESH,
         )
 
@@ -188,20 +190,20 @@
         ref = gathered.at[chunk(origin_of(d, k), core, piece), :]
         pltpu.make_async_remote_copy(
             src_ref=ref, dst_ref=ref,
-            send_sem=ring_send.at[d, k - 1, piece], recv_sem=ring_recv.at[d, k - 1, piece],
+            send_sem=row_send, recv_sem=ring_recv.at[d, k - 1, piece],
             device_id=along_y(leg if d == 0 else -leg), device_id_type=MESH,
         ).wait_recv()
 
     def sib_copy(i, origin, piece, cc):
         ref = gathered.at[chunk(origin, cc, piece), :]
         return pltpu.make_async_remote_copy(
-            src_ref=ref, dst_ref=ref, send_sem=sib_send.at[i], recv_sem=sib_recv.at[i],
+            src_ref=ref, dst_ref=ref, send_sem=row_send, recv_sem=sib_recv.at[i],
             device_id=sib_id, device_id_type=MESH,
         )
 
-    def plane_wait(dz):
-        for dx in range(NX):
-            plane_copy(dz * NX + dx).wait_recv()
+    def plane_wait(part):
+        blocks = landed.at[pl.ds(0, 15 + part)]
+        pltpu.make_async_copy(blocks, blocks, plane_recv.at[part]).wait()
 
     def start_piece(piece):
         for i in range(2):
@@ -213,17 +215,13 @@
         gathered[chunk(y, core, piece), :] = packed[...].astype(jnp.bfloat16)
         for k in (2, 1):
             for d in range(2):
-                launch(ring_copy(piece, d, k))
-
-    for dx in range(1, NX):
-        plane_copy(dx).wait_recv()
-    for dz in (1, 7, 2 + 4 * odd):
-        plane_wait(dz)
+                ring_copy(piece, d, k).start()
+
+    plane_wait(0)
     start_piece(0)
-    for dz in (6 - 4 * odd, 3, 5, 4):
-        plane_wait(dz)
+    plane_wait(1)
     start_piece(1)
-    launch(sib_copy(0, y, None, core))
+    sib_copy(0, y, None, core).start()
     ready_queries()
     attend(0, 16)
     send_partials()
@@ -267,14 +265,14 @@
             arrived(piece, d, k)
             if k == 2:
                 if d == 1 - piece:
-                    launch(ring_copy(piece, d, 4))
-                launch(ring_copy(piece, d, 3))
+                    ring_copy(piece, d, 4).start()
+                ring_copy(piece, d, 3).start()
         if k == 4:
-            launch(sib_copy(LAST + piece, origin_of(0, 4), piece, core))
+            sib_copy(LAST + piece, origin_of(0, 4), piece, core).start()
 
     def share(k):
         for d in range(2):
-            launch(sib_copy(2 * k - 1 + d, origin_of(d, k), None, core))
+            sib_copy(2 * k - 1 + d, origin_of(d, k), None, core).start()
 
     projected = jnp.zeros((16, QB), jnp.float32)
     receive(0, 2)
@@ -297,7 +295,6 @@
         projected = process(5 + d, origin_of(d, 3), projected)
 
     partial_copy.wait_recv()
-    merged = []
     for h in range(HEADS):
         own = osc[pl.ds(h, 16, stride=8), :]
         ml = mlsc[pl.ds(h, 16, stride=8), :]
@@ -307,13 +304,9 @@
         joint = jnp.maximum(own_peak, peer_peak)
         own_factor = jnp.exp(own_peak - joint)
         peer_factor = jnp.exp(peer_peak - joint)
-        merged.append(
-            (
-                joint,
-                own_total * own_factor + peer_total * peer_factor,
-                own * own_factor + precv[h] * peer_factor,
-            )
-        )
+        merged[0, h] = jnp.broadcast_to(joint, (16, QB))
+        merged[1, h] = jnp.broadcast_to(own_total * own_factor + peer_total * peer_factor, (16, QB))
+        merged[2, h] = own * own_factor + precv[h] * peer_factor
     projected = process(LAST, origin_of(0, 4), projected)
 
     rotated = projected * cosine + pltpu.roll(projected, 64, 1) * sine
@@ -323,13 +316,17 @@
     scale_out[...] = jnp.transpose(scale_v[...], (1, 0))[0:1, 0:40]
     for copy in sends:
         copy.wait_send()
+    blocks = landed.at[pl.ds(0, 31)]
+    pltpu.make_async_copy(blocks, blocks, plane_send).wait()
+    rows = gathered.at[pl.ds(0, 4800), :]
+    pltpu.make_async_copy(rows, rows, row_send).wait()
     entry_copy.wait()
     own = esend[...].astype(jnp.float32)
     other = erecv[...].astype(jnp.float32)
     key = jnp.where(half == 1, other, own)
     value = jnp.where(half == 1, own, other)
     for h in range(HEADS):
-        joint, total, weighted = merged[h]
+        joint, total, weighted = merged[0, h], merged[1, h], merged[2, h]
         q_h = q_v[:, h * QB:(h + 1) * QB].astype(jnp.float32)
         score = jnp.sum(q_h * key, axis=1, keepdims=True) / root
         peak = jnp.maximum(joint, score)
@@ -392,12 +389,12 @@
             pltpu.VMEM((HEADS + 1, rows, QB), f32),
             pltpu.VMEM((rows, QB), bf16),
             pltpu.VMEM((rows, QB), bf16),
+            pltpu.VMEM((3, HEADS, rows, QB), f32),
             dma((8,)),
-            dma((NZ * NX,)),
-            dma((NZ * NX,)),
+            dma,
+            dma((2,)),
+            dma,
             dma((2, 4, 2)),
-            dma((2, 4, 2)),
-            dma((9,)),
             dma((9,)),
             dma((3,)),
             dma((3,)),

time: 38 us -> 37 us (0.974)
  Pallas kernels: 37.2 us -> 36.2 us
    pallas_call x1, Pallas kernels: 36 us -> 35.1 us  [shards(): pl.pallas_call(kernel, out_shape=(pltpu.VMEM((depth, QB), bf16), pltpu.VM...]
where the time goes in v4:
time: 37 us; the launch traced here: 36.8 us
  Pallas kernels  36.2 us (98%)
  between operations  0.64 us (2%)
    pallas_call x1, Pallas kernels, shards(): pl.pallas_call(kernel, out_shape=(pltpu.VMEM((depth, QB), bf16), pltpu.VM...  35.1 us
    pallas_call x1, Pallas kernels, shards(): pl.pallas_call(settle, out_shape=(jax.ShapeDtypeStruct((depth, QB), bf16)...  1.11 us

profile of v4, /device:TPU:1, one launch (start us, length us, event | category | flops | bytes accessed | tf_op | source)
XLA Modules:
  0.0 36.8 jit_solution(11970905282106444970)
XLA Ops:
  0.6 35.1 %sync_decode.1 = (bf16[5120,128]{1,0:T(8,128)(2,1)S(1)}, f32[1,40]{1,0:T(1,128)S(1)}, bf16[16,512]{1,0:T(8,128)(2,1)S(1)}) custom-call(bf16[10,2048]{1,0:T(8,128)(2,1)} %w_hbm.1, bf16[16,5120]{1,0:T(8,128)(2,1)} %hid_hbm.1, bf16[16,512]{1,0:T(8,128)(2,1)} %q_hbm.1, s32[16,1,128,128]{3,2,1,0:T(8,128)} %kc_hbm.1, f32[16,1,128]{2,1,0:T(1,128)} %ks_hbm.1, ...), custom_call_target="tpu_custom_call" | custom-call | flops 60000000 | bytes 6000000 | tf_op jit(solution)/shard_map/sync_decode/pallas_call | solution.py:360
  35.7 1.1 %settle.1 = (bf16[5120,128]{1,0:T(8,128)(2,1)}, f32[1,40]{1,0:T(1,128)}, bf16[16,512]{1,0:T(8,128)(2,1)}) custom-call(bf16[5120,128]{1,0:T(8,128)(2,1)S(1)} %get-tuple-element.9.synced, f32[1,40]{1,0:T(1,128)S(1)} %get-tuple-element.10.scales, bf16[16,512]{1,0:T(8,128)(2,1)S(1)} %get-tuple-element.11.attended), custom_call_target="tpu_custom_call" | custom-call | tf_op jit(solution)/shard_map/settle/pallas_call | solution.py:408

commit v5 on v4

--- a/solution.py
+++ b/solution.py
@@ -181,7 +181,7 @@
         ref = gathered.at[chunk(origin_of(d, k - leg), core, piece), :]
         return pltpu.make_async_remote_copy(
             src_ref=ref, dst_ref=ref,
-            send_sem=row_send, recv_sem=ring_recv.at[d, k - 1, piece],
+            send_sem=row_send, recv_sem=ring_recv.at[d, k - 1, piece or 0],
             device_id=along_y(leg if d == 0 else -leg), device_id_type=MESH,
         )
 
@@ -190,7 +190,7 @@
         ref = gathered.at[chunk(origin_of(d, k), core, piece), :]
         pltpu.make_async_remote_copy(
             src_ref=ref, dst_ref=ref,
-            send_sem=row_send, recv_sem=ring_recv.at[d, k - 1, piece],
+            send_sem=row_send, recv_sem=ring_recv.at[d, k - 1, piece or 0],
             device_id=along_y(leg if d == 0 else -leg), device_id_type=MESH,
         ).wait_recv()
 
@@ -213,14 +213,15 @@
                         (2 * pairs[2 * piece + i] + side) * NX + e
                     ].astype(jnp.float32)
         gathered[chunk(y, core, piece), :] = packed[...].astype(jnp.bfloat16)
-        for k in (2, 1):
-            for d in range(2):
-                ring_copy(piece, d, k).start()
+        for d in range(2):
+            ring_copy(piece, d, 2).start()
 
     plane_wait(0)
     start_piece(0)
     plane_wait(1)
     start_piece(1)
+    for d in range(2):
+        ring_copy(None, d, 1).start()
     sib_copy(0, y, None, core).start()
     ready_queries()
     attend(0, 16)
@@ -276,10 +277,10 @@
 
     projected = jnp.zeros((16, QB), jnp.float32)
     receive(0, 2)
-    receive(0, 1)
     receive(1, 2)
     share(2)
-    receive(1, 1)
+    for d in range(2):
+        arrived(None, d, 1)
     share(1)
     projected = process(0, y, projected)
     receive(0, 3)

time: 37 us -> 37 us (level)
  no operation moved by 1% of the time
where the time goes in v5:
time: 37 us; the launch traced here: 36.9 us
  Pallas kernels  36.2 us (98%)
  between operations  0.64 us (2%)
    pallas_call x1, Pallas kernels, shards(): pl.pallas_call(kernel, out_shape=(pltpu.VMEM((depth, QB), bf16), pltpu.VM...  35.1 us
    pallas_call x1, Pallas kernels, shards(): pl.pallas_call(settle, out_shape=(jax.ShapeDtypeStruct((depth, QB), bf16)...  1.11 us

profile of v5, /device:TPU:1, one launch (start us, length us, event | category | flops | bytes accessed | tf_op | source)
XLA Modules:
  0.0 36.9 jit_solution(16482525979594050157)
XLA Ops:
  0.6 35.1 %sync_decode.1 = (bf16[5120,128]{1,0:T(8,128)(2,1)S(1)}, f32[1,40]{1,0:T(1,128)S(1)}, bf16[16,512]{1,0:T(8,128)(2,1)S(1)}) custom-call(bf16[10,2048]{1,0:T(8,128)(2,1)} %w_hbm.1, bf16[16,5120]{1,0:T(8,128)(2,1)} %hid_hbm.1, bf16[16,512]{1,0:T(8,128)(2,1)} %q_hbm.1, s32[16,1,128,128]{3,2,1,0:T(8,128)} %kc_hbm.1, f32[16,1,128]{2,1,0:T(1,128)} %ks_hbm.1, ...), custom_call_target="tpu_custom_call" | custom-call | flops 60000000 | bytes 6000000 | tf_op jit(solution)/shard_map/sync_decode/pallas_call | solution.py:361
  35.7 1.1 %settle.1 = (bf16[5120,128]{1,0:T(8,128)(2,1)}, f32[1,40]{1,0:T(1,128)}, bf16[16,512]{1,0:T(8,128)(2,1)}) custom-call(bf16[5120,128]{1,0:T(8,128)(2,1)S(1)} %get-tuple-element.9.synced, f32[1,40]{1,0:T(1,128)S(1)} %get-tuple-element.10.scales, bf16[16,512]{1,0:T(8,128)(2,1)S(1)} %get-tuple-element.11.attended), custom_call_target="tpu_custom_call" | custom-call | tf_op jit(solution)/shard_map/settle/pallas_call | solution.py:409

commit v6 on v4

--- a/solution.py
+++ b/solution.py
@@ -176,12 +176,15 @@
     def origin_of(d, k):
         return (y + NY - k) % NY if d == 0 else (y + k) % NY
 
+    def ring_slot(piece, d, k):
+        return {1: d, 3: 2 + d}[k] if k % 2 else {2: 4 + 2 * d, 4: 8}[k] + piece
+
     def ring_copy(piece, d, k):
         leg = 2 if k % 2 == 0 else 1
         ref = gathered.at[chunk(origin_of(d, k - leg), core, piece), :]
         return pltpu.make_async_remote_copy(
             src_ref=ref, dst_ref=ref,
-            send_sem=row_send, recv_sem=ring_recv.at[d, k - 1, piece],
+            send_sem=row_send, recv_sem=ring_recv.at[ring_slot(piece, d, k)],
             device_id=along_y(leg if d == 0 else -leg), device_id_type=MESH,
         )
 
@@ -190,7 +193,7 @@
         ref = gathered.at[chunk(origin_of(d, k), core, piece), :]
         pltpu.make_async_remote_copy(
             src_ref=ref, dst_ref=ref,
-            send_sem=row_send, recv_sem=ring_recv.at[d, k - 1, piece],
+            send_sem=row_send, recv_sem=ring_recv.at[ring_slot(piece, d, k)],
             device_id=along_y(leg if d == 0 else -leg), device_id_type=MESH,
         ).wait_recv()
 
@@ -276,16 +279,16 @@
 
     projected = jnp.zeros((16, QB), jnp.float32)
     receive(0, 2)
-    receive(0, 1)
     receive(1, 2)
     share(2)
-    receive(1, 1)
+    for d in range(2):
+        arrived(None, d, 1)
     share(1)
     projected = process(0, y, projected)
-    receive(0, 3)
     for d in range(2):
         projected = process(3 + d, origin_of(d, 2), projected)
-    receive(1, 3)
+    for d in range(2):
+        arrived(None, d, 3)
     share(3)
     for d in range(2):
         projected = process(1 + d, origin_of(d, 1), projected)
@@ -394,7 +397,7 @@
             dma,
             dma((2,)),
             dma,
-            dma((2, 4, 2)),
+            dma((10,)),
             dma((9,)),
             dma((3,)),
             dma((3,)),

time: 37 us -> 36.9 us (level)
  no operation moved by 1% of the time
where the time goes in v6:
time: 36.9 us; the launch traced here: 36.8 us
  Pallas kernels  36.1 us (98%)
  between operations  0.64 us (2%)
    pallas_call x1, Pallas kernels, shards(): pl.pallas_call(kernel, out_shape=(pltpu.VMEM((depth, QB), bf16), pltpu.VM...  35 us
    pallas_call x1, Pallas kernels, shards(): pl.pallas_call(settle, out_shape=(jax.ShapeDtypeStruct((depth, QB), bf16)...  1.11 us

profile of v6, /device:TPU:1, one launch (start us, length us, event | category | flops | bytes accessed | tf_op | source)
XLA Modules:
  0.0 36.8 jit_solution(12449183427729937219)
XLA Ops:
  0.6 35.0 %sync_decode.1 = (bf16[5120,128]{1,0:T(8,128)(2,1)S(1)}, f32[1,40]{1,0:T(1,128)S(1)}, bf16[16,512]{1,0:T(8,128)(2,1)S(1)}) custom-call(bf16[10,2048]{1,0:T(8,128)(2,1)} %w_hbm.1, bf16[16,5120]{1,0:T(8,128)(2,1)} %hid_hbm.1, bf16[16,512]{1,0:T(8,128)(2,1)} %q_hbm.1, s32[16,1,128,128]{3,2,1,0:T(8,128)} %kc_hbm.1, f32[16,1,128]{2,1,0:T(1,128)} %ks_hbm.1, ...), custom_call_target="tpu_custom_call" | custom-call | flops 60000000 | bytes 6000000 | tf_op jit(solution)/shard_map/sync_decode/pallas_call | solution.py:363
  35.6 1.1 %settle.1 = (bf16[5120,128]{1,0:T(8,128)(2,1)}, f32[1,40]{1,0:T(1,128)}, bf16[16,512]{1,0:T(8,128)(2,1)}) custom-call(bf16[5120,128]{1,0:T(8,128)(2,1)S(1)} %get-tuple-element.9.synced, f32[1,40]{1,0:T(1,128)S(1)} %get-tuple-element.10.scales, bf16[16,512]{1,0:T(8,128)(2,1)S(1)} %get-tuple-element.11.attended), custom_call_target="tpu_custom_call" | custom-call | tf_op jit(solution)/shard_map/settle/pallas_call | solution.py:411
